TPU v7x, 256 devices: a whole 4x4x8 slice. The times are simulated.
256 devices in a mesh: row: 8 (over z), col: 32 (over x, y, core).
Axes of the slice: x: 4, y: 4, z: 8, core: 2. Of those that a mesh axis runs over, the one named last changes fastest.
Arguments:
- gradient: bfloat16 [16384, 16384], P('row', 'col'), may hold values from -6 to 6
- momentum: bfloat16 [16384, 16384], P('row', 'col'), may hold values from -6 to 6
- right_factor: float32 [16384, 256], P('col'), may hold values from -12 to 12
- weight: bfloat16 [16384, 16384], P('row', 'col'), may hold values from -6 to 6
Outputs:
- new_weight: bfloat16 [16384, 16384], P('row', 'col')
- new_momentum: bfloat16 [16384, 16384], P('row', 'col')
- new_factor: float32 [16384, 256], P('col')
All inputs are finite; a program needn't handle non-finite values.
Results may differ from a plain program's by a relative error of at most 0.015.
Values may be sent and summed in bfloat16 or wider, within the bound.
A program may use at most 64 MiB of HBM per device.

v0:
```python
import jax
import jax.numpy as jnp
from jax import lax
from jax.sharding import PartitionSpec as P

ROWS = 16384
COLS = 16384
RANK = 256


momentum_keep = 0.6
step_size = 0.1


def contract_rows(first, second, exact):
    if exact:
        return lax.dot_general(
            first,
            second,
            (((0,), (0,)), ((), ())),
            precision=lax.Precision.HIGHEST,
            preferred_element_type=jnp.float32,
        )
    return lax.dot_general(
        first, second, (((0,), (0,)), ((), ())), preferred_element_type=jnp.float32
    )


def apply_lower(gram, left):
    lower = jnp.linalg.cholesky(gram)
    return lax.linalg.triangular_solve(lower, left, left_side=False, lower=True, transpose_a=True)


def local(gradient, momentum, right_factor, weight):
    blended = (momentum.astype(jnp.float32) + gradient.astype(jnp.float32)).astype(jnp.bfloat16)
    partial_left = jnp.dot(
        blended, right_factor.astype(jnp.bfloat16), preferred_element_type=jnp.float32
    )
    left = lax.psum(partial_left, "col")
    gram = lax.psum(contract_rows(left, left, True), "row")
    ortho = apply_lower(gram, left)
    left_half = ortho.astype(jnp.bfloat16)
    right = lax.psum(contract_rows(blended, left_half, False).astype(jnp.bfloat16), "row").astype(
        jnp.float32
    )
    column_sums = lax.psum(jnp.sum(right * right, axis=0), "col")
    new_factor = right * lax.rsqrt(column_sums / COLS + 1e-06)
    right_half = right.astype(jnp.bfloat16)
    projection = jnp.dot(left_half, right_half.T, preferred_element_type=jnp.float32)
    new_momentum = (blended.astype(jnp.float32) - (1.0 - momentum_keep) * projection).astype(
        jnp.bfloat16
    )
    new_half = new_factor.astype(jnp.bfloat16)
    direction = jnp.dot(left_half, new_half.T, preferred_element_type=jnp.float32)
    scaled = step_size * (ROWS / RANK) ** 0.5
    new_weight = (weight.astype(jnp.float32) - scaled * direction).astype(jnp.bfloat16)
    return (new_weight, new_momentum, new_factor)


def solution(mesh):
    return jax.shard_map(
        local,
        mesh=mesh,
        in_specs=(P("row", "col"), P("row", "col"), P("col", None), P("row", "col")),
        out_specs=(P("row", "col"), P("row", "col"), P("col", None)),
        check_vma=False,
    )
```

profile of v0, /device:TPU:1, one launch (start us, length us, event | category | flops | bytes accessed | tf_op | source)
XLA Modules:
  0.0 428.1 jit_solution(13605739779203349187)
XLA Ops:
  7.2 4.3 %fusion.5 = f32[2048,256]{1,0:T(8,128)} fusion(f32[512,256]{1,0:T(8,128)} %param.6, bf16[2048,512]{1,0:T(8,128)(2,1)} %param.4, bf16[2048,512]{1,0:T(8,128)(2,1)} %param.5), kind=kOutput, calls=%fused_computation.20 | convolution fusion | flops 541196288 | bytes 6815744 | tf_op jit(solution)/shard_map/dot_general | solution.py:36
  11.6 121.5 %all-reduce.5.cloned.1.call-done = f32[2048,256]{1,0:T(8,128)} async-done(((f32[2048,256]{1,0:T(8,128)}), f32[2048,256]{1,0:T(8,128)}) %all-reduce.5.cloned.1.call-update) | async-done | bytes 2097168 | tf_op jit(solution)/shard_map/psum | solution.py:39
  133.1 6.4 %fusion.16 = f32[256,256]{0,1:T(8,128)} fusion(f32[2048,256]{1,0:T(8,128)} %all-reduce.5.cloned.1.call-done), kind=kOutput, calls=%fused_computation.44 | convolution fusion | flops 1610612736 | bytes 2359296 | tf_op jit(solution)/shard_map/dot_general | solution.py:17
  139.7 67.7 %all-reduce.7.cloned.1.call-done = f32[256,256]{0,1:T(8,128)} async-done(((f32[256,256]{0,1:T(8,128)}), f32[256,256]{0,1:T(8,128)}) %all-reduce.7.cloned.1.call-update) | async-done | bytes 262160 | tf_op jit(solution)/shard_map/psum | solution.py:40
  207.4 1.1 copy.8
  208.5 1.0 fusion.3
  209.5 11.7 %cholesky.50 = f32[128,128]{1,0:T(8,128)S(1)} custom-call(f32[128,128]{1,0:T(8,128)S(1)} %cholesky.118), custom_call_target="Cholesky" | custom-call | tf_op jit(solution)/shard_map/jit(cholesky)/cholesky | solution.py:30
  221.3 9.8 %custom-call.14 = f32[1,128,128]{1,2,0:T(8,128)S(1)} custom-call(f32[1,128,128]{2,1,0:T(8,128)S(1)} %get-tuple-element.24), custom_call_target="InvertDiagBlocksLowerTriangular" | custom-call | tf_op jit(solution)/shard_map/jit(cholesky)/cholesky | solution.py:30
  231.6 11.7 %cholesky.105 = f32[128,128]{1,0:T(8,128)S(1)} custom-call(f32[128,128]{1,0:T(8,128)S(1)} %convolution_subtract_fusion.1), custom_call_target="Cholesky" | custom-call | tf_op jit(solution)/shard_map/jit(cholesky)/cholesky | solution.py:30
  243.4 0.6 compare_reduce_fusion
  245.4 4.2 while.1
  246.2 1.4 bitcast_dynamic-update-slice_fusion.2
  248.2 1.4 bitcast_dynamic-update-slice_fusion.2
  249.6 19.7 %custom-call.15 = f32[2,128,128]{1,2,0:T(8,128)S(1)} custom-call(f32[2,128,128]{2,1,0:T(8,128)S(1)} %get-tuple-element.10), custom_call_target="InvertDiagBlocksLowerTriangular" | custom-call | tf_op jit(solution)/shard_map/triangular_solve | solution.py:31
  269.3 1.1 fusion.15
  270.4 1.8 convolution_subtract_fusion
  272.2 1.1 convolution_convert_fusion
  273.3 1.5 convolution_convert_fusion.1
  274.8 71.1 %all-reduce.9.cloned.1.call-done = bf16[512,256]{1,0:T(8,128)(2,1)} async-done(((bf16[512,256]{1,0:T(8,128)(2,1)}), bf16[512,256]{1,0:T(8,128)(2,1)}) %all-reduce.9.cloned.1.call-update) | async-done | bytes 262160 | tf_op jit(solution)/shard_map/psum | solution.py:43
  345.9 1.0 fusion.2
  347.0 67.2 %psum.31 = f32[256]{0:T(256)S(1)} all-reduce(f32[256]{0:T(256)S(1)} %fusion.2), channel_id=1, replica_groups=mesh['row'=8,'col'=32] {'col'}, use_global_device_ids=true, to_apply=%region_8.9 | all-reduce | flops 256 | bytes 2048 | tf_op jit(solution)/shard_map/psum | solution.py:46
  414.2 1.0 convert_multiply_fusion
  415.2 3.9 subtract_convert_fusion.1
  419.1 2.5 subtract_convert_fusion
  (35 shorter events, 2.3 us)
Async XLA Ops:
  7.2 125.9 %all-reduce.5.cloned.1.call-start = ((), (), s32[]{:S(2)}) async-start(), calls=%async_computation | async-start | bytes 4194304 | tf_op jit(solution)/shard_map/psum | solution.py:39
  11.6 195.9 %all-reduce.7.cloned.1.call-start = ((), (), s32[]{:S(2)}) async-start(), calls=%async_computation.1 | async-start | bytes 524288 | tf_op jit(solution)/shard_map/psum | solution.py:40
  139.5 129.8 %copy-start = (f32[2048,256]{1,0:T(8,128)S(1)}, f32[2048,256]{1,0:T(8,128)}, u32[]{:S(2)}) copy-start(f32[2048,256]{1,0:T(8,128)} %all-reduce.5.cloned.1.call-done) | copy-start | bytes 6291460
  139.5 206.4 %all-reduce.9.cloned.1.call-start = ((), (), s32[]{:S(2)}) async-start(), calls=%async_computation.2 | async-start | bytes 524288 | tf_op jit(solution)/shard_map/psum | solution.py:43
  270.4 2.9 copy-start.1
  270.4 2.9 copy-start.3
  415.2 3.9 copy-start.6
  415.2 3.9 copy-start.2
  415.2 3.9 copy-start.4
  415.2 3.9 copy-start.5
Sparse Core Ops, SparseCore 0:
  11.8 121.1 all-reduce.4
  139.6 67.7 all-reduce.6
  275.0 70.8 all-reduce.8
where the time goes:
time: 428 us
  waiting for transfers between devices  260 us (61%)
  blocking collectives  67.2 us (16%)
  other arithmetic  56.7 us (13%)
  matrix products  23 us (5%)
  between operations  15.2 us (4%)
  local copies, waits for them, and re-layouts  5.16 us (1%)
    psum x1, waiting for transfers between devices, local(): left = lax.psum(partial_left, 'col')  121 us
    psum x1, waiting for transfers between devices, local(): lax.psum(contract_rows(blended, left_half, False).astype(jnp.bfloat16), '...  71.1 us
    psum x1, waiting for transfers between devices, local(): gram = lax.psum(contract_rows(left, left, True), 'row')  67.7 us
    psum x1, blocking collectives, local(): column_sums = lax.psum(jnp.sum(right * right, axis=0), 'col')  67.2 us
    another operation x6, other arithmetic, apply_lower(): lower = jnp.linalg.cholesky(gram)  34 us
    another operation x3, other arithmetic, apply_lower(): lax.linalg.triangular_solve(lower, left, left_side=False, lower=True, tra...  19.7 us
  transfers between devices with their start and end apart: 3, of which 3 were waited for; matrix products, arithmetic and copies ran while one was open for 0% of the time, Pallas kernels for 0%

commit v1 on v0

v1 whole, which is shorter than its diff:
```python
import functools

import jax
import jax.numpy as jnp
from jax import lax
from jax.experimental import pallas as pl
from jax.experimental.pallas import tpu as pltpu
from jax.sharding import PartitionSpec as P

ROWS = 16384
COLS = 16384
RANK = 256
CORES = 2
NX = 4
NY = 4

momentum_keep = 0.6
step_size = 0.1

F32 = jnp.float32
BF16 = jnp.bfloat16
MESH = pl.DeviceIdType.MESH


def split3(value):
    high = value.astype(BF16)
    rest = value - high.astype(F32)
    middle = rest.astype(BF16)
    return high, middle, (rest - middle.astype(F32)).astype(BF16)


def inverse_factor(gram_ref, work_ref, out_ref, size=32, group=16):
    n = gram_ref.shape[0]
    tiles_across = n // 128
    gram = gram_ref[...]
    rows = lax.broadcasted_iota(jnp.int32, (n, n), 0)
    cols = lax.broadcasted_iota(jnp.int32, (n, n), 1)
    diagonal = jnp.where(rows == cols, gram, 0.0)
    scale_row = lax.rsqrt(jnp.sum(diagonal, axis=0, keepdims=True))
    scale_col = lax.rsqrt(jnp.sum(diagonal, axis=1, keepdims=True))
    work_ref[:, :n] = gram * scale_row * scale_col
    work_ref[:, n:] = jnp.where(rows == cols, 1.0, 0.0)

    def block(j, carry):
        start = pl.multiple_of(j * size, size)
        outer = pl.multiple_of((j // (128 // size)) * 128, 128)
        lead = work_ref[pl.ds(start, size), pl.ds(outer, 128)]
        lead = pltpu.roll(lead, lax.rem(128 - (start - outer), 128), 1)
        panel = work_ref[pl.ds(start, size), :]
        tiles = [lead] + [panel[:, t * 128 : (t + 1) * 128] for t in range(2 * tiles_across)]
        done = []
        for first in range(0, size, group):
            height = size - first
            sub = lax.broadcasted_iota(jnp.int32, (height, 128), 0)
            top = sub[:group]
            lead = tiles[0]
            columns = [
                jnp.broadcast_to(lead[:, first + i : first + i + 1], (height, 128))
                for i in range(group)
            ]
            scale = jnp.ones((group, 128), F32)
            for k in range(0, group, 2):
                one, two = columns[k], columns[k + 1]
                a = one[k : k + 1, :]
                b = one[k + 1 : k + 2, :]
                c = two[k + 1 : k + 2, :]
                det = a * c - b * b
                inv_a = 1.0 / a
                inv_det = 1.0 / det
                m1 = (one * c - two * b) * inv_det
                m2 = (two * a - one * b) * inv_det
                m1 = jnp.where(sub > k + 1, m1, jnp.where(sub == k + 1, b * inv_a, 0.0))
                m2 = jnp.where(sub > k + 1, m2, 0.0)
                scale = jnp.where(
                    top == k,
                    lax.rsqrt(a),
                    jnp.where(top == k + 1, lax.rsqrt(det * inv_a), scale),
                )
                for i in range(k + 2, group):
                    old = columns[i]
                    columns[i] = old - m1 * old[k : k + 1, :] - m2 * old[k + 1 : k + 2, :]
                tiles = [t - m1 * t[k : k + 1, :] - m2 * t[k + 1 : k + 2, :] for t in tiles]
            done.append([t[:group] * scale for t in tiles[1:]])
            tiles = [t[group:] for t in tiles]
        tiles = [jnp.concatenate([d[t] for d in done], axis=0) for t in range(2 * tiles_across)]
        left = jnp.concatenate(tiles[:tiles_across], axis=1)
        right = jnp.concatenate(tiles[tiles_across:], axis=1)
        out_ref[pl.ds(start, size), :] = right * scale_row

        @pl.when(j < n // size - 1)
        def _():
            lane = lax.broadcasted_iota(jnp.int32, (size, n), 1)
            rest = jnp.where(lane >= start + size, left, 0.0)
            ph, pm, pq = split3(rest)
            xh, xm, xq = split3(right)
            lhs = jnp.concatenate([ph, ph, pm, pm, ph, pq], axis=0)
            rhs_g = jnp.concatenate([ph, pm, ph, pm, pq, ph], axis=0)
            rhs_x = jnp.concatenate([xh, xm, xh, xm, xq, xh], axis=0)
            rhs = jnp.concatenate([rhs_g, rhs_x], axis=1)
            work_ref[...] -= lax.dot_general(
                lhs, rhs, (((0,), (0,)), ((), ())), preferred_element_type=F32
            )

        return carry

    lax.fori_loop(0, n // size, block, 0)


def factor_kernel(
    nx,
    ny,
    nz,
    cols_total,
    g_hbm,
    m_hbm,
    v_hbm,
    la_out,
    lb_out,
    z1_out,
    z2_out,
    nf_out,
    g_v,
    m_v,
    v_v,
    b_v,
    xs,
    xr,
    s_v,
    sa,
    sb,
    ra1,
    rb1,
    ta,
    tb,
    ta_h,
    tb_h,
    ra2,
    rb2,
    la,
    lb,
    gfull,
    gz,
    gall,
    wh,
    wr,
    wg,
    work,
    inv,
    cs,
    z1,
    z2,
    nf,
    load_sem,
    out_sem,
    pair_s,
    pair_r,
    a1_s,
    a1_r,
    b1_s,
    b1_r,
    a2_s,
    a2_r,
    b2_s,
    b2_r,
    ga1_s,
    ga1_r,
    gb1_s,
    gb1_r,
    ga2_s,
    ga2_r,
    gb2_s,
    gb2_r,
    fa_s,
    fa_r,
    fb_s,
    fb_r,
    gz_s,
    gz_r,
    gp_s,
    gp_r,
    wr_s,
    wr_r,
    wg_s,
    wg_r,
    cs_s,
    cs_r,
):
    z = lax.axis_index("row")
    p = lax.axis_index("col")
    core = lax.rem(p, CORES)
    y = lax.rem(p // CORES, ny)
    x = p // (CORES * ny)
    plane = nx * ny * CORES
    rank = v_v.shape[1]
    half_rank = rank // 2
    half = b_v.shape[0] // CORES
    quarter = half // 2

    def at(x_to, y_to, core_to):
        return {"row": z, "col": (x_to * ny + y_to) * CORES + core_to}

    def send(src, dst, s_sem, r_sem, to):
        return pltpu.make_async_remote_copy(
            src_ref=src, dst_ref=dst, send_sem=s_sem, recv_sem=r_sem,
            device_id=to, device_id_type=MESH,
        )

    offsets = [(1 - core) * half, (1 - core) * half + quarter, core * half, core * half + quarter]
    offsets = [pl.multiple_of(o, quarter) for o in offsets]
    v_load = pltpu.make_async_copy(v_hbm, v_v, load_sem.at[8])
    v_load.start()
    loads = []
    for q, offset in enumerate(offsets):
        part = pl.ds(offset, quarter)
        pair = [
            pltpu.make_async_copy(g_hbm.at[part], g_v.at[part], load_sem.at[2 * q]),
            pltpu.make_async_copy(m_hbm.at[part], m_v.at[part], load_sem.at[2 * q + 1]),
        ]
        for c in pair:
            c.start()
        loads.append(pair)

    barrier = pltpu.get_barrier_semaphore()

    def greet_plane(d, carry):
        pl.semaphore_signal(
            barrier, inc=1, device_id={"row": z, "col": lax.rem(p + d, plane)}, device_id_type=MESH
        )
        return carry

    def greet_line(d, carry):
        pl.semaphore_signal(
            barrier, inc=1, device_id={"row": lax.rem(z + d, nz), "col": p}, device_id_type=MESH
        )
        return carry

    lax.fori_loop(1, plane, greet_plane, 0)
    lax.fori_loop(1, nz, greet_line, 0)

    v_load.wait()
    factor_half = v_v[...].astype(BF16)
    pair_copies = []
    for q, offset in enumerate(offsets):
        for c in loads[q]:
            c.wait()
        part = pl.ds(offset, quarter)
        blended = (m_v[part, :].astype(F32) + g_v[part, :].astype(F32)).astype(BF16)
        b_v[part, :] = blended
        product = jnp.dot(blended, factor_half, preferred_element_type=F32)
        if q < 2:
            xs[q] = product.astype(BF16)
            if q == 0:
                pl.semaphore_wait(barrier, plane - 1 + nz - 1)
            copy = send(xs.at[q], xr.at[q], pair_s.at[q], pair_r.at[q], at(x, y, 1 - core))
            copy.start()
            pair_copies.append(copy)
        else:
            s_v[pl.ds((q - 2) * quarter, quarter), :] = product

    chunk = half // (nx * ny)
    slab = chunk * ny
    for q in range(2):
        pair_copies[q].wait_recv()
        total = s_v[pl.ds(q * quarter, quarter), :] + xr[q].astype(F32)
        s_v[pl.ds(q * quarter, quarter), :] = total
        per = nx // 2
        for i in range(per):
            xi = q * per + i
            rows = total[i * slab : (i + 1) * slab, :].astype(BF16)
            sa[xi] = rows[:, :half_rank].reshape(ny, chunk, half_rank)
            sb[:, xi] = rows[:, half_rank:].reshape(ny, chunk, half_rank)
    a1, b1 = [], []
    for d in range(1, nx):
        to = lax.rem(x + d, nx)
        c = send(sa.at[to], ra1.at[d - 1], a1_s.at[d - 1], a1_r.at[d - 1], at(to, y, core))
        c.start()
        a1.append(c)
    for d in range(1, ny):
        to = lax.rem(y + d, ny)
        c = send(sb.at[to], rb1.at[d - 1], b1_s.at[d - 1], b1_r.at[d - 1], at(x, to, core))
        c.start()
        b1.append(c)
    acc = s_v[pl.ds(pl.multiple_of(x * slab, slab), slab), :half_rank].reshape(ny, chunk, half_rank)
    for d in range(1, nx):
        a1[d - 1].wait_recv()
        acc = acc + ra1[d - 1].astype(F32)
    ta[...] = acc
    ta_h[...] = acc.astype(BF16)
    a2, b2 = [], []
    for d in range(1, ny):
        to = lax.rem(y + d, ny)
        c = send(ta_h.at[to], ra2.at[d - 1], a2_s.at[d - 1], a2_r.at[d - 1], at(x, to, core))
        c.start()
        a2.append(c)
    for d in range(1, ny):
        b1[d - 1].wait_recv()
    for xi in range(nx):
        own = s_v[pl.ds(pl.multiple_of(xi * slab + y * chunk, chunk), chunk), half_rank:]
        for d in range(1, ny):
            own = own + rb1[d - 1, xi].astype(F32)
        tb[xi] = own
        tb_h[xi] = own.astype(BF16)
    for d in range(1, nx):
        to = lax.rem(x + d, nx)
        c = send(tb_h.at[to], rb2.at[d - 1], b2_s.at[d - 1], b2_r.at[d - 1], at(to, y, core))
        c.start()
        b2.append(c)

    acc = ta[y]
    for d in range(1, ny):
        a2[d - 1].wait_recv()
        acc = acc + ra2[d - 1].astype(F32)
    la[core, x, y] = acc.astype(BF16)
    ga1, gb1, ga2, gb2, fa, fb = [], [], [], [], [], []
    for d in range(1, ny):
        to = lax.rem(y + d, ny)
        here = la.at[core, x, y]
        c = send(here, here, ga1_s.at[d - 1], ga1_r.at[d - 1], at(x, to, core))
        c.start()
        ga1.append(c)
    acc = tb[x]
    for d in range(1, nx):
        b2[d - 1].wait_recv()
        acc = acc + rb2[d - 1].astype(F32)
    lb[core, x, y] = acc.astype(BF16)
    for d in range(1, nx):
        to = lax.rem(x + d, nx)
        here = lb.at[core, x, y]
        c = send(here, here, gb1_s.at[d - 1], gb1_r.at[d - 1], at(to, y, core))
        c.start()
        gb1.append(c)

    def forward_a(slot, x_of):
        here = la.at[core, x_of]
        c = send(here, here, fa_s.at[slot], fa_r.at[slot], at(x, y, 1 - core))
        c.start()
        fa.append(c)

    def forward_b(slot, y_of):
        here = lb.at[core, :, y_of]
        c = send(here, here, fb_s.at[slot], fb_r.at[slot], at(x, y, 1 - core))
        c.start()
        fb.append(c)

    for c in ga1:
        c.wait_recv()
    for d in range(1, nx):
        to = lax.rem(x + d, nx)
        here = la.at[core, x]
        c = send(here, here, ga2_s.at[d - 1], ga2_r.at[d - 1], at(to, y, core))
        c.start()
        ga2.append(c)
    forward_a(0, x)
    for c in gb1:
        c.wait_recv()
    for d in range(1, ny):
        to = lax.rem(y + d, ny)
        here = lb.at[core, :, y]
        c = send(here, here, gb2_s.at[d - 1], gb2_r.at[d - 1], at(x, to, core))
        c.start()
        gb2.append(c)
    forward_b(0, y)
    for d in range(1, max(nx, ny)):
        if d < nx:
            ga2[d - 1].wait_recv()
            forward_a(d, lax.rem(x + nx - d, nx))
        if d < ny:
            gb2[d - 1].wait_recv()
            forward_b(d, lax.rem(y + ny - d, ny))
    for c in fa + fb:
        c.wait_recv()

    outs = [
        pltpu.make_async_copy(la, la_out, out_sem.at[0]),
        pltpu.make_async_copy(lb, lb_out, out_sem.at[1]),
    ]
    for c in outs:
        c.start()

    n_rows = half * CORES
    left = jnp.concatenate(
        [la[...].reshape(n_rows, half_rank), lb[...].reshape(n_rows, half_rank)], axis=1
    )
    left_t = left.T
    gfull[...] = jnp.dot(left_t, left, preferred_element_type=F32)
    share = rank // plane
    mine = pl.ds(pl.multiple_of(p * share, share), share)
    gz[z] = gfull[mine, :]
    gz_c = []
    for d in range(1, nz):
        to = lax.rem(z + d, nz)
        c = send(gz.at[z], gz.at[z], gz_s.at[d - 1], gz_r.at[d - 1], {"row": to, "col": p})
        c.start()
        gz_c.append(c)

    w = jnp.dot(left_t, b_v[...], preferred_element_type=F32).astype(BF16)
    line = rank // nz
    wh[...] = w.reshape(nz, line, w.shape[1])
    wr[z] = wh[z]
    wr_c = []
    for d in range(1, nz):
        to = lax.rem(z + d, nz)
        c = send(wh.at[to], wr.at[z], wr_s.at[d - 1], wr_r.at[d - 1], {"row": to, "col": p})
        c.start()
        wr_c.append(c)

    for c in gz_c:
        c.wait_recv()
    acc = gz[0]
    for i in range(1, nz):
        acc = acc + gz[i]
    gall[mine, :] = acc

    def spread(d, carry):
        send(gall.at[mine], gall.at[mine], gp_s, gp_r, {"row": z, "col": lax.rem(p + d, plane)}).start()
        return carry

    lax.fori_loop(1, plane, spread, 0)

    for c in wr_c:
        c.wait_recv()
    acc = wr[0].astype(F32)
    for i in range(1, nz):
        acc = acc + wr[i].astype(F32)
    wg[z] = acc.astype(BF16)
    wg_c = []
    for d in range(1, nz):
        to = lax.rem(z + d, nz)
        c = send(wg.at[z], wg.at[z], wg_s.at[d - 1], wg_r.at[d - 1], {"row": to, "col": p})
        c.start()
        wg_c.append(c)

    others = gall.at[pl.ds(0, (plane - 1) * share)]
    all_gram = send(others, others, gp_s, gp_r, at(x, y, 1 - core))
    all_gram.wait_recv()
    inverse_factor(gall, work, inv)

    for c in wg_c:
        c.wait_recv()
    w = wg[...].reshape(rank, w.shape[1])
    high, middle, _ = split3(inv[...])
    right_t = jnp.dot(high, w, preferred_element_type=F32) + jnp.dot(
        middle, w, preferred_element_type=F32
    )
    squares = right_t * right_t
    sq_h, sq_m, _ = split3(squares)
    ones = jnp.ones((8, w.shape[1]), BF16)
    dims = (((1,), (1,)), ((), ()))
    cs[p] = lax.dot_general(ones, sq_h, dims, preferred_element_type=F32) + lax.dot_general(
        ones, sq_m, dims, preferred_element_type=F32
    )

    def spread_sums(d, carry):
        send(cs.at[p], cs.at[p], cs_s, cs_r, {"row": z, "col": lax.rem(p + d, plane)}).start()
        return carry

    lax.fori_loop(1, plane, spread_sums, 0)
    inv_t = inv[...].T
    right_half = right_t.astype(BF16)
    z1[...] = jnp.dot(inv_t.astype(BF16), right_half, preferred_element_type=F32).astype(BF16)
    right = right_t.T
    other_sums = cs.at[pl.ds(0, plane - 1)]
    all_sums = send(other_sums, other_sums, cs_s, cs_r, at(x, y, 1 - core))
    all_sums.wait_recv()
    acc = cs[0]
    for i in range(1, plane):
        acc = acc + cs[i]
    scale = lax.rsqrt(acc / cols_total + 1e-06)[0:1, :]
    z2[...] = jnp.dot(
        (inv_t * scale).astype(BF16), right_half, preferred_element_type=F32
    ).astype(BF16)
    nf[...] = right * scale
    last = [
        pltpu.make_async_copy(z1, z1_out, out_sem.at[2]),
        pltpu.make_async_copy(z2, z2_out, out_sem.at[3]),
        pltpu.make_async_copy(nf, nf_out, out_sem.at[4]),
    ]
    for c in last:
        c.start()
    for c in outs + last:
        c.wait()
    for c in pair_copies + a1 + b1 + a2 + b2 + ga1 + gb1 + ga2 + gb2 + fa + fb + gz_c + wr_c + wg_c:
        c.wait_send()
    all_gram.wait_send()
    all_sums.wait_send()


def update_kernel(scaled, g_ref, m_ref, w_ref, la_ref, lb_ref, z1_ref, z2_ref, nf_ref, nw_ref, nm_ref, out_ref):
    blended = (m_ref[...].astype(F32) + g_ref[...].astype(F32)).astype(BF16)
    left = jnp.concatenate([la_ref[...], lb_ref[...]], axis=1)
    projection = jnp.dot(left, z1_ref[...], preferred_element_type=F32)
    nm_ref[...] = (blended.astype(F32) - (1.0 - momentum_keep) * projection).astype(BF16)
    direction = jnp.dot(left, z2_ref[...], preferred_element_type=F32)
    nw_ref[...] = (w_ref[...].astype(F32) - scaled * direction).astype(BF16)
    out_ref[...] = nf_ref[...]


def local(nx, ny, nz, cols_total, scaled, gradient, momentum, right_factor, weight):
    n_rows, n_cols = gradient.shape
    rank = right_factor.shape[1]
    half_rank = rank // 2
    half = n_rows // CORES
    quarter = half // 2
    chunk = half // (nx * ny)
    plane = nx * ny * CORES
    share = rank // plane
    line = rank // nz
    any_spec = pl.BlockSpec(memory_space=pl.ANY)
    dma = pltpu.SemaphoreType.DMA
    vm = pltpu.VMEM
    scratch = [
        vm((n_rows, n_cols), BF16),
        vm((n_rows, n_cols), BF16),
        vm((n_cols, rank), F32),
        vm((n_rows, n_cols), BF16),
        vm((2, quarter, rank), BF16),
        vm((2, quarter, rank), BF16),
        vm((half, rank), F32),
        vm((nx, ny, chunk, half_rank), BF16),
        vm((ny, nx, chunk, half_rank), BF16),
        vm((nx - 1, ny, chunk, half_rank), BF16),
        vm((ny - 1, nx, chunk, half_rank), BF16),
        vm((ny, chunk, half_rank), F32),
        vm((nx, chunk, half_rank), F32),
        vm((ny, chunk, half_rank), BF16),
        vm((nx, chunk, half_rank), BF16),
        vm((ny - 1, chunk, half_rank), BF16),
        vm((nx - 1, chunk, half_rank), BF16),
        vm((CORES, nx, ny, chunk, half_rank), BF16),
        vm((CORES, nx, ny, chunk, half_rank), BF16),
        vm((rank, rank), F32),
        vm((nz, share, rank), F32),
        vm((rank, rank), F32),
        vm((nz, line, n_cols), BF16),
        vm((nz, line, n_cols), BF16),
        vm((nz, line, n_cols), BF16),
        vm((rank, 2 * rank), F32),
        vm((rank, rank), F32),
        vm((plane, 8, rank), F32),
        vm((rank, n_cols), BF16),
        vm((rank, n_cols), BF16),
        vm((n_cols, rank), F32),
        dma((9,)),
        dma((5,)),
        dma((2,)), dma((2,)),
        dma((nx - 1,)), dma((nx - 1,)), dma((ny - 1,)), dma((ny - 1,)),
        dma((ny - 1,)), dma((ny - 1,)), dma((nx - 1,)), dma((nx - 1,)),
        dma((ny - 1,)), dma((ny - 1,)), dma((nx - 1,)), dma((nx - 1,)),
        dma((nx - 1,)), dma((nx - 1,)), dma((ny - 1,)), dma((ny - 1,)),
        dma((nx,)), dma((nx,)), dma((ny,)), dma((ny,)),
        dma((nz - 1,)), dma((nz - 1,)),
        dma, dma,
        dma((nz - 1,)), dma((nz - 1,)),
        dma((nz - 1,)), dma((nz - 1,)),
        dma, dma,
    ]
    gathered = jax.ShapeDtypeStruct((CORES, nx, ny, chunk, half_rank), BF16)
    thin = jax.ShapeDtypeStruct((rank, n_cols), BF16)
    la, lb, z1, z2, nf = pl.pallas_call(
        functools.partial(factor_kernel, nx, ny, nz, cols_total),
        out_shape=[gathered, gathered, thin, thin, jax.ShapeDtypeStruct((n_cols, rank), F32)],
        in_specs=[any_spec] * 3,
        out_specs=[any_spec] * 5,
        scratch_shapes=scratch,
        compiler_params=pltpu.CompilerParams(
            collective_id=0, has_side_effects=True, vmem_limit_bytes=32 * 1024 * 1024
        ),
        name="factors",
    )(gradient, momentum, right_factor)
    la = la.reshape(n_rows, half_rank)
    lb = lb.reshape(n_rows, half_rank)
    steps = 8
    block = n_rows // steps
    piece = n_cols // steps
    rows_spec = pl.BlockSpec((block, n_cols), lambda i: (i, 0))
    left_spec = pl.BlockSpec((block, half_rank), lambda i: (i, 0))
    whole = pl.BlockSpec((rank, n_cols), lambda i: (0, 0))
    nf_spec = pl.BlockSpec((piece, rank), lambda i: (i, 0))
    return pl.pallas_call(
        functools.partial(update_kernel, scaled),
        grid=(steps,),
        out_shape=[
            jax.ShapeDtypeStruct((n_rows, n_cols), BF16),
            jax.ShapeDtypeStruct((n_rows, n_cols), BF16),
            jax.ShapeDtypeStruct((n_cols, rank), F32),
        ],
        in_specs=[rows_spec] * 3 + [left_spec] * 2 + [whole] * 2 + [nf_spec],
        out_specs=[rows_spec, rows_spec, nf_spec],
        compiler_params=pltpu.CompilerParams(vmem_limit_bytes=24 * 1024 * 1024),
        name="update",
    )(gradient, momentum, weight, la, lb, z1, z2, nf)


def build(mesh, nx, ny, nz, cols_total, rows_total, rank):
    scaled = step_size * (rows_total / rank) ** 0.5
    return jax.shard_map(
        functools.partial(local, nx, ny, nz, cols_total, scaled),
        mesh=mesh,
        in_specs=(P("row", "col"), P("row", "col"), P("col", None), P("row", "col")),
        out_specs=(P("row", "col"), P("row", "col"), P("col", None)),
        check_vma=False,
    )


def solution(mesh):
    return build(mesh, NX, NY, mesh.shape["row"], COLS, ROWS, RANK)
```

time: 428 us -> 69.8 us (0.16)
  waiting for transfers between devices: 260 us -> 0 us
  blocking collectives: 67.2 us -> 0 us
  Pallas kernels: 0 us -> 64.8 us
  other arithmetic: 56.7 us -> 0 us
  matrix products: 23 us -> 0 us
  between operations: 15.2 us -> 0.66 us
    psum x3 -> x0, waiting for transfers between devices: 260 us -> none  [the longest x1 121 us: local(): left = lax.psum(partial_left, 'col')]
    psum x1 -> x0, blocking collectives: 67.2 us -> none  [local(): column_sums = lax.psum(jnp.sum(right * right, axis=0), 'col')]
    pallas_call x0 -> x2, Pallas kernels: none -> 64.8 us  [the longest x1 60.1 us: local(): pl.pallas_call(functools.partial(factor_kernel, nx, ny, nz, cols_total),...]
    another operation x9 -> x0, other arithmetic: 53.7 us -> none  [the longest x6 34 us: apply_lower(): lower = jnp.linalg.cholesky(gram)]
    dot_general x5 -> x0, matrix products: 18.6 us -> none  [the longest x1 6.38 us: contract_rows(): lax.dot_general(first, second, (((0,), (0,)), ((), ())), precision=lax.Pr...]
    another operation x5 -> x0, matrix products: 4.44 us -> none  [the longest x3 3.97 us: apply_lower(): lax.linalg.triangular_solve(lower, left, left_side=False, lower=True, tra...]
  transfers between devices with their start and end apart: 3 -> 0, of which waited for: 3 -> 0; matrix products, arithmetic and copies ran while one was open for 0% -> 0% of each run, Pallas kernels for 0% -> 0%
where the time goes in v1:
time: 69.8 us; the launch traced here: 69.6 us
  Pallas kernels  64.8 us (93%)
  local copies, waits for them, and re-layouts  4.22 us (6%)
    pallas_call x1, Pallas kernels, local(): pl.pallas_call(functools.partial(factor_kernel, nx, ny, nz, cols_total),...  60.1 us
    pallas_call x1, Pallas kernels, local(): pl.pallas_call(functools.partial(update_kernel, scaled), grid=(steps,), o...  4.65 us
    unnamed x8, local copies, waits for them, and re-layouts  4.22 us

profile of v1, /device:TPU:1, one launch (start us, length us, event | category | flops | bytes accessed | tf_op | source)
XLA Modules:
  0.0 69.6 jit_solution(6920036984272258499)
XLA Ops:
  0.6 0.0 copy-start
  0.6 1.6 %copy-done = bf16[2048,512]{1,0:T(8,128)(2,1)S(1)} copy-done((bf16[2048,512]{1,0:T(8,128)(2,1)S(1)}, bf16[2048,512]{1,0:T(8,128)(2,1)}, u32[]{:S(2)}) %copy-start) | copy-done | bytes 2097176
  2.2 0.0 copy-start.1
  2.2 1.6 %copy-done.1 = bf16[2048,512]{1,0:T(8,128)(2,1)S(1)} copy-done((bf16[2048,512]{1,0:T(8,128)(2,1)S(1)}, bf16[2048,512]{1,0:T(8,128)(2,1)}, u32[]{:S(2)}) %copy-start.1) | copy-done | bytes 2097176
  3.8 0.0 copy-start.3
  3.8 1.0 %copy-done.3 = f32[512,256]{1,0:T(8,128)S(1)} copy-done((f32[512,256]{1,0:T(8,128)S(1)}, f32[512,256]{1,0:T(8,128)}, u32[]{:S(2)}) %copy-start.3) | copy-done | bytes 524312
  4.9 0.0 copy-start.2
  4.9 60.1 %factors.1 = (bf16[2,4,4,64,128]{4,3,2,1,0:T(8,128)(2,1)S(1)}, bf16[2,4,4,64,128]{4,3,2,1,0:T(8,128)(2,1)S(1)}, bf16[256,512]{1,0:T(8,128)(2,1)S(1)}, bf16[256,512]{1,0:T(8,128)(2,1)S(1)}, f32[512,256]{1,0:T(8,128)S(1)}) custom-call(bf16[2048,512]{1,0:T(8,128)(2,1)S(1)} %copy-done, bf16[2048,512]{1,0:T(8,128)(2,1)S(1)} %copy-done.1, f32[512,256]{1,0:T(8,128)S(1)} %copy-done.3), custom_call_target="tpu_custom_call" | custom-call | tf_op jit(solution)/shard_map/factors/pallas_call | solution.py:559
  65.0 0.0 copy-done.2
  65.0 4.7 %update.1 = (bf16[2048,512]{1,0:T(8,128)(2,1)}, bf16[2048,512]{1,0:T(8,128)(2,1)}, f32[512,256]{1,0:T(8,128)}) custom-call(bf16[2048,512]{1,0:T(8,128)(2,1)S(1)} %copy-done, bf16[2048,512]{1,0:T(8,128)(2,1)S(1)} %copy-done.1, bf16[2048,512]{1,0:T(8,128)(2,1)S(1)} %copy-done.2, bf16[2048,128]{1,0:T(8,128)(2,1)S(1)} %bitcast.2, bf16[2048,128]{1,0:T(8,128)(2,1)S(1)} %bitcast.3, ...), custom_call_target="tpu_custom_call" | custom-call | tf_op jit(solution)/shard_map/update/pallas_call | solution.py:579
Async XLA Ops:
  0.6 1.6 %copy-start = (bf16[2048,512]{1,0:T(8,128)(2,1)S(1)}, bf16[2048,512]{1,0:T(8,128)(2,1)}, u32[]{:S(2)}) copy-start(bf16[2048,512]{1,0:T(8,128)(2,1)} %g_ref.1) | copy-start | bytes 6291460
  2.2 1.6 %copy-start.1 = (bf16[2048,512]{1,0:T(8,128)(2,1)S(1)}, bf16[2048,512]{1,0:T(8,128)(2,1)}, u32[]{:S(2)}) copy-start(bf16[2048,512]{1,0:T(8,128)(2,1)} %m_ref.1) | copy-start | bytes 6291460
  3.8 1.0 %copy-start.3 = (f32[512,256]{1,0:T(8,128)S(1)}, f32[512,256]{1,0:T(8,128)}, u32[]{:S(2)}) copy-start(f32[512,256]{1,0:T(8,128)} %v_hbm.1) | copy-start | bytes 1572868
  4.9 60.1 %copy-start.2 = (bf16[2048,512]{1,0:T(8,128)(2,1)S(1)}, bf16[2048,512]{1,0:T(8,128)(2,1)}, u32[]{:S(2)}) copy-start(bf16[2048,512]{1,0:T(8,128)(2,1)} %w_ref.1) | copy-start | bytes 6291460

commit v2 on v0

v2 whole, which is shorter than its diff:
```python
import functools

import jax
import jax.numpy as jnp
from jax import lax
from jax.experimental import pallas as pl
from jax.experimental.pallas import tpu as pltpu
from jax.sharding import PartitionSpec as P

ROWS = 16384
COLS = 16384
RANK = 256
CORES = 2
sum_pieces = 2
piece_rows = 16
steps = 8
NX = 4
NY = 4

momentum_keep = 0.6
step_size = 0.1

F32 = jnp.float32
BF16 = jnp.bfloat16
MESH = pl.DeviceIdType.MESH


def split3(value):
    high = value.astype(BF16)
    rest = value - high.astype(F32)
    middle = rest.astype(BF16)
    return high, middle, (rest - middle.astype(F32)).astype(BF16)


def inverse_factor(gram_ref, work_ref, out_ref, size=32, group=16):
    n = gram_ref.shape[0]
    tiles_across = n // 128
    gram = gram_ref[...]
    rows = lax.broadcasted_iota(jnp.int32, (n, n), 0)
    cols = lax.broadcasted_iota(jnp.int32, (n, n), 1)
    diagonal = jnp.where(rows == cols, gram, 0.0)
    scale_row = lax.rsqrt(jnp.sum(diagonal, axis=0, keepdims=True))
    scale_col = lax.rsqrt(jnp.sum(diagonal, axis=1, keepdims=True))
    work_ref[:, :n] = gram * scale_row * scale_col
    work_ref[:, n:] = jnp.where(rows == cols, 1.0, 0.0)

    def block(j, carry):
        start = pl.multiple_of(j * size, size)
        outer = pl.multiple_of((j // (128 // size)) * 128, 128)
        lead = work_ref[pl.ds(start, size), pl.ds(outer, 128)]
        lead = pltpu.roll(lead, lax.rem(128 - (start - outer), 128), 1)
        panel = work_ref[pl.ds(start, size), :]
        tiles = [lead] + [panel[:, t * 128 : (t + 1) * 128] for t in range(2 * tiles_across)]
        done = []
        for first in range(0, size, group):
            height = size - first
            sub = lax.broadcasted_iota(jnp.int32, (height, 128), 0)
            top = sub[:group]
            lead = tiles[0]
            columns = [
                jnp.broadcast_to(lead[:, first + i : first + i + 1], (height, 128))
                for i in range(group)
            ]
            scale = jnp.ones((group, 128), F32)
            for k in range(0, group, 2):
                one, two = columns[k], columns[k + 1]
                a = one[k : k + 1, :]
                b = one[k + 1 : k + 2, :]
                c = two[k + 1 : k + 2, :]
                det = a * c - b * b
                inv_a = 1.0 / a
                inv_det = 1.0 / det
                m1 = (one * c - two * b) * inv_det
                m2 = (two * a - one * b) * inv_det
                m1 = jnp.where(sub > k + 1, m1, jnp.where(sub == k + 1, b * inv_a, 0.0))
                m2 = jnp.where(sub > k + 1, m2, 0.0)
                scale = jnp.where(
                    top == k,
                    lax.rsqrt(a),
                    jnp.where(top == k + 1, lax.rsqrt(det * inv_a), scale),
                )
                for i in range(k + 2, group):
                    old = columns[i]
                    columns[i] = old - m1 * old[k : k + 1, :] - m2 * old[k + 1 : k + 2, :]
                tiles = [t - m1 * t[k : k + 1, :] - m2 * t[k + 1 : k + 2, :] for t in tiles]
            done.append([t[:group] * scale for t in tiles[1:]])
            tiles = [t[group:] for t in tiles]
        tiles = [jnp.concatenate([d[t] for d in done], axis=0) for t in range(2 * tiles_across)]
        left = jnp.concatenate(tiles[:tiles_across], axis=1)
        right = jnp.concatenate(tiles[tiles_across:], axis=1)
        out_ref[pl.ds(start, size), :] = right * scale_row

        @pl.when(j < n // size - 1)
        def _():
            lane = lax.broadcasted_iota(jnp.int32, (size, n), 1)
            rest = jnp.where(lane >= start + size, left, 0.0)
            ph, pm, pq = split3(rest)
            xh, xm, xq = split3(right)
            lhs = jnp.concatenate([ph, ph, pm, pm, ph, pq], axis=0)
            rhs_g = jnp.concatenate([ph, pm, ph, pm, pq, ph], axis=0)
            rhs_x = jnp.concatenate([xh, xm, xh, xm, xq, xh], axis=0)
            rhs = jnp.concatenate([rhs_g, rhs_x], axis=1)
            work_ref[...] -= lax.dot_general(
                lhs, rhs, (((0,), (0,)), ((), ())), preferred_element_type=F32
            )

        return carry

    lax.fori_loop(0, n // size, block, 0)


def factor_kernel(nx, ny, nz, cols_total, g_hbm, m_hbm, v_hbm, *refs):
    b_outs, l_outs, refs = refs[:steps], refs[steps : 2 * steps], refs[2 * steps :]
    z1_out, xt_out, r_out, r2_out, scale_out, g_v, m_v, v_v, b_v, xs, xr, s_v, sa, ra, la, *refs = refs
    lt, gfull, gz, gall, wacc, wh, wr, wg, work, inv, cs, z1, xt, right, scale_v, *refs = refs
    load_sem, out_sem, pair_s, pair_r, rs_s, rs_r, ag_s, ag_r, fw_s, fw_r, *refs = refs
    gz_s, gz_r, gp_s, gp_r, wr_s, wr_r, wg_s, wg_r, cs_s, cs_r = refs
    z = lax.axis_index("row")
    p = lax.axis_index("col")
    core = lax.rem(p, CORES)
    q = p // CORES
    chips = nx * ny
    plane = chips * CORES
    rank = v_v.shape[1]
    half_rank = rank // 2
    n_cols = b_v.shape[1]
    half = b_v.shape[0] // CORES
    n_pieces, piece = xs.shape[0], xs.shape[1]

    def at(chip_to, core_to):
        return {"row": z, "col": chip_to * CORES + core_to}

    sent = []

    def copy_to(src, dst, s_sem, r_sem, to):
        return pltpu.make_async_remote_copy(
            src_ref=src,
            dst_ref=dst,
            send_sem=s_sem,
            recv_sem=r_sem,
            device_id=to,
            device_id_type=MESH,
        )

    def send(src, dst, s_sem, r_sem, to):
        copy = copy_to(src, dst, s_sem, r_sem, to)
        copy.start()
        sent.append(copy)
        return copy

    barrier = pltpu.get_barrier_semaphore()

    def greet_plane(d, carry):
        to = {"row": z, "col": lax.rem(p + d, plane)}
        pl.semaphore_signal(barrier, inc=1, device_id=to, device_id_type=MESH)
        return carry

    def greet_line(d, carry):
        to = {"row": lax.rem(z + d, nz), "col": p}
        pl.semaphore_signal(barrier, inc=1, device_id=to, device_id_type=MESH)
        return carry

    lax.fori_loop(1, plane, greet_plane, 0)
    lax.fori_loop(1, nz, greet_line, 0)
    v_load = pltpu.make_async_copy(v_hbm, v_v, load_sem.at[0])
    v_load.start()
    offsets = [(1 - core) * half + h * piece for h in range(n_pieces)]
    offsets += [core * half + h * piece for h in range(n_pieces)]
    offsets = [pl.multiple_of(o, piece) for o in offsets]
    loads = []
    for i, offset in enumerate(offsets):
        part = pl.ds(offset, piece)
        pair = [
            pltpu.make_async_copy(g_hbm.at[part], g_v.at[part], load_sem.at[2 * i + 1]),
            pltpu.make_async_copy(m_hbm.at[part], m_v.at[part], load_sem.at[2 * i + 2]),
        ]
        for c in pair:
            c.start()
        loads.append(pair)
    v_load.wait()
    factor_half = v_v[...].astype(BF16)

    def product(i):
        for c in loads[i]:
            c.wait()
        part = pl.ds(offsets[i], piece)
        blended = (m_v[part, :].astype(F32) + g_v[part, :].astype(F32)).astype(BF16)
        b_v[part, :] = blended
        return jnp.dot(blended, factor_half, preferred_element_type=F32)

    for h in range(n_pieces):
        xs[h] = product(h).astype(BF16)
    pl.semaphore_wait(barrier, plane - 1 + nz - 1)
    pairs = []
    for h in range(n_pieces):
        pairs.append(send(xs.at[h], xr.at[h], pair_s.at[h], pair_r.at[h], at(q, 1 - core)))

    def spread_piece(h):
        def to_chip(d, carry):
            to = lax.rem(q + d, chips)
            copy_to(sa.at[h, to], ra.at[h, q], rs_s.at[h], rs_r.at[h], at(to, core)).start()
            return carry

        lax.fori_loop(1, chips, to_chip, 0)

    for h in range(n_pieces):
        own = product(n_pieces + h)
        ra[h, q] = jnp.zeros((piece_rows, rank), BF16)
        pairs[h].wait_recv()
        total = (own + xr[h].astype(F32)).reshape(chips, piece_rows, rank)
        s_v[h] = total
        sa[h] = total.astype(BF16)
        spread_piece(h)

    def gather_piece(h):
        def to_chip(d, carry):
            to = lax.rem(q + d, chips)
            here = la.at[core, h, q]
            copy_to(here, here, ag_s.at[h], ag_r.at[h], at(to, core)).start()
            return carry

        lax.fori_loop(1, chips, to_chip, 0)

    waits = []
    for h in range(n_pieces):
        slots = ra.at[h, pl.ds(0, chips - 1)]
        arrived = copy_to(slots, slots, rs_s.at[h], rs_r.at[h], at(q, 1 - core))
        arrived.wait_recv()
        waits.append(arrived)
        la[core, h, q] = (s_v[h, q] + jnp.sum(ra[h].astype(F32), axis=0)).astype(BF16)
        gather_piece(h)

    def accumulate(h):
        forwards[h].wait_recv()
        for c in range(CORES):
            rows = la[c, h].reshape(piece, rank)
            rows_t = rows.T
            first = (c * n_pieces + h) * piece
            lt[:, first : first + piece] = rows_t
            update = jnp.dot(rows_t, rows, preferred_element_type=F32)
            gfull[...] = update if h == 0 and c == 0 else gfull[...] + update

    def accumulate_right(h):
        for c in range(CORES):
            first = (c * n_pieces + h) * piece
            update = jnp.dot(
                lt[:, first : first + piece],
                b_v[first : first + piece, :],
                preferred_element_type=F32,
            )
            wacc[...] = update if h == 0 and c == 0 else wacc[...] + update

    forwards = []
    for h in range(n_pieces):
        slots = la.at[core, h, pl.ds(0, chips - 1)]
        arrived = copy_to(slots, slots, ag_s.at[h], ag_r.at[h], at(q, 1 - core))
        arrived.wait_recv()
        waits.append(arrived)
        here = la.at[core, h]
        forwards.append(send(here, here, fw_s.at[h], fw_r.at[h], at(q, 1 - core)))
        if h > 0:
            accumulate(h - 1)
    for h in range(n_pieces - 1):
        accumulate_right(h)
    accumulate(n_pieces - 1)

    share = rank // plane
    mine = pl.ds(pl.multiple_of(p * share, share), share)
    gz[z] = gfull[mine, :]
    gz_c = []
    for d in range(1, nz):
        to = {"row": lax.rem(z + d, nz), "col": p}
        gz_c.append(send(gz.at[z], gz.at[z], gz_s.at[d - 1], gz_r.at[d - 1], to))

    accumulate_right(n_pieces - 1)
    w = wacc[...].astype(BF16)
    line = rank // nz
    part = line // sum_pieces
    wh[...] = w.reshape(nz, sum_pieces, part, n_cols)
    wr_c = []
    for h in range(sum_pieces):
        wr[h, z] = wh[z, h]
        for d in range(1, nz):
            to = lax.rem(z + d, nz)
            sems = wr_s.at[h, d - 1], wr_r.at[h, d - 1]
            wr_c.append(send(wh.at[to, h], wr.at[h, z], *sems, {"row": to, "col": p}))
    outs = []
    for i in range(steps):
        rows = b_v.shape[0] // steps
        c, h = i * rows // half, (i * rows % half) // piece
        chip = (i * rows % piece) // piece_rows
        source = la.at[c, h, pl.ds(chip, rows // piece_rows)]
        outs.append(pltpu.make_async_copy(source, l_outs[i], out_sem.at[2 * i]))
        source = b_v.at[pl.ds(i * rows, rows)]
        outs.append(pltpu.make_async_copy(source, b_outs[i], out_sem.at[2 * i + 1]))
    for c in outs:
        c.start()

    for c in gz_c:
        c.wait_recv()
    acc = gz[0]
    for i in range(1, nz):
        acc = acc + gz[i]
    gall[mine, :] = acc

    def spread(d, carry):
        to = {"row": z, "col": lax.rem(p + d, plane)}
        copy_to(gall.at[mine], gall.at[mine], gp_s, gp_r, to).start()
        return carry

    lax.fori_loop(1, plane, spread, 0)

    wg_c = []
    for h in range(sum_pieces):
        for c in wr_c[h * (nz - 1) : (h + 1) * (nz - 1)]:
            c.wait_recv()
        acc = wr[h, 0].astype(F32)
        for i in range(1, nz):
            acc = acc + wr[h, i].astype(F32)
        wg[z, h] = acc.astype(BF16)
        for d in range(1, nz):
            to = {"row": lax.rem(z + d, nz), "col": p}
            sems = wg_s.at[h, d - 1], wg_r.at[h, d - 1]
            wg_c.append(send(wg.at[z, h], wg.at[z, h], *sems, to))

    others = gall.at[pl.ds(0, (plane - 1) * share)]
    all_gram = copy_to(others, others, gp_s, gp_r, at(q, 1 - core))
    all_gram.wait_recv()
    inverse_factor(gall, work, inv)
    inv_t = inv[...].T.astype(BF16)
    xt[...] = inv_t
    outs.append(pltpu.make_async_copy(xt, xt_out, out_sem.at[2 * steps]))
    outs[-1].start()

    for c in wg_c:
        c.wait_recv()
    w = wg[...].reshape(rank, n_cols)
    high, middle, _ = split3(inv[...])
    right_t = jnp.dot(high, w, preferred_element_type=F32) + jnp.dot(
        middle, w, preferred_element_type=F32
    )
    squares = right_t * right_t
    sq_h, sq_m, _ = split3(squares)
    ones = jnp.ones((8, n_cols), BF16)
    dims = (((1,), (1,)), ((), ()))
    sums = lax.dot_general(ones, sq_h, dims, preferred_element_type=F32) + lax.dot_general(
        ones, sq_m, dims, preferred_element_type=F32
    )
    upper = lax.broadcasted_iota(jnp.int32, (8, half_rank), 0) < 4
    cs[p] = jnp.where(upper, sums[:, :half_rank], sums[:, half_rank:])

    def spread_sums(d, carry):
        to = {"row": z, "col": lax.rem(p + d, plane)}
        copy_to(cs.at[p], cs.at[p], cs_s, cs_r, to).start()
        return carry

    lax.fori_loop(1, plane, spread_sums, 0)
    z1[...] = jnp.dot(inv_t, right_t.astype(BF16), preferred_element_type=F32).astype(BF16)
    right[...] = right_t.T
    mid = n_cols // 2
    outs += [
        pltpu.make_async_copy(z1, z1_out, out_sem.at[2 * steps + 1]),
        pltpu.make_async_copy(right.at[pl.ds(0, mid)], r_out, out_sem.at[2 * steps + 2]),
        pltpu.make_async_copy(right.at[pl.ds(mid, mid)], r2_out, out_sem.at[2 * steps + 3]),
    ]
    for c in outs[-3:]:
        c.start()
    for c in sent + waits + [all_gram]:
        c.wait_send()
    other_sums = cs.at[pl.ds(0, plane - 1)]
    all_sums = copy_to(other_sums, other_sums, cs_s, cs_r, at(q, 1 - core))
    all_sums.wait_recv()
    acc = cs[0]
    for i in range(1, plane):
        acc = acc + cs[i]
    acc = lax.rsqrt(acc / cols_total + 1e-06)
    scale = jnp.concatenate([acc[0:1, :], acc[4:5, :]], axis=1)
    scale_v[...] = jnp.broadcast_to(scale, scale_v.shape)
    outs.append(pltpu.make_async_copy(scale_v, scale_out, out_sem.at[2 * steps + 4]))
    outs[-1].start()
    for c in outs:
        c.wait()
    all_sums.wait_send()


def update_kernel(scaled, *refs):
    b_refs, l_refs, refs = refs[:steps], refs[steps : 2 * steps], refs[2 * steps :]
    w_ref, z1_ref, xt_ref, r_ref, r2_ref, scale_ref, nw_hbm, nm_hbm, nf_hbm, nw, nm, nf, sems = refs
    block = nw.shape[0] // steps
    mid = r_ref.shape[0]
    scale = scale_ref[0:1, :]
    nf[:mid, :] = r_ref[...] * scale
    nf[mid:, :] = r2_ref[...] * scale
    copies = [pltpu.make_async_copy(nf, nf_hbm, sems.at[2 * steps])]
    copies[0].start()
    z2 = lax.dot_general(
        xt_ref[...],
        nf[...].astype(BF16),
        (((1,), (1,)), ((), ())),
        preferred_element_type=F32,
    ).astype(BF16)
    for i in range(steps):
        part = pl.ds(i * block, block)
        left = l_refs[i][...].reshape(block, z2.shape[0])
        projection = jnp.dot(left, z1_ref[...], preferred_element_type=F32)
        nm[part, :] = (b_refs[i][...].astype(F32) - (1.0 - momentum_keep) * projection).astype(BF16)
        copies.append(pltpu.make_async_copy(nm.at[part], nm_hbm.at[part], sems.at[2 * i]))
        copies[-1].start()
        direction = jnp.dot(left, z2, preferred_element_type=F32)
        nw[part, :] = (w_ref[part, :].astype(F32) - scaled * direction).astype(BF16)
        copies.append(pltpu.make_async_copy(nw.at[part], nw_hbm.at[part], sems.at[2 * i + 1]))
        copies[-1].start()
    for c in copies:
        c.wait()


def local(nx, ny, nz, cols_total, scaled, gradient, momentum, right_factor, weight):
    n_rows, n_cols = gradient.shape
    rank = right_factor.shape[1]
    half = n_rows // CORES
    chips = nx * ny
    piece = chips * piece_rows
    n_pieces = half // piece
    plane = chips * CORES
    share = rank // plane
    part = rank // nz // sum_pieces
    block = n_rows // steps
    any_spec = pl.BlockSpec(memory_space=pl.ANY)
    vm_spec = pl.BlockSpec(memory_space=pltpu.VMEM)
    dma = pltpu.SemaphoreType.DMA
    vm = pltpu.VMEM
    shape = jax.ShapeDtypeStruct
    rows = (n_pieces, chips, piece_rows, rank)
    scratch = [
        vm((n_rows, n_cols), BF16),
        vm((n_rows, n_cols), BF16),
        vm((n_cols, rank), F32),
        vm((n_rows, n_cols), BF16),
        vm((n_pieces, piece, rank), BF16),
        vm((n_pieces, piece, rank), BF16),
        vm(rows, F32),
        vm(rows, BF16),
        vm(rows, BF16),
        vm((CORES,) + rows, BF16),
        vm((rank, n_rows), BF16),
        vm((rank, rank), F32),
        vm((nz, share, rank), F32),
        vm((rank, rank), F32),
        vm((rank, n_cols), F32),
        vm((nz, sum_pieces, part, n_cols), BF16),
        vm((sum_pieces, nz, part, n_cols), BF16),
        vm((nz, sum_pieces, part, n_cols), BF16),
        vm((rank, 2 * rank), F32),
        vm((rank, rank), F32),
        vm((plane, 8, rank // 2), F32),
        vm((rank, n_cols), BF16),
        vm((rank, rank), BF16),
        vm((n_cols, rank), F32),
        vm((8, rank), F32),
        dma((4 * n_pieces + 1,)),
        dma((2 * steps + 5,)),
    ]
    scratch += [dma((n_pieces,))] * 8
    scratch += [dma((nz - 1,)), dma((nz - 1,)), dma, dma]
    scratch += [dma((sum_pieces, nz - 1))] * 4 + [dma, dma]
    outs = [shape((block, n_cols), BF16)] * steps
    outs += [shape((block // piece_rows, piece_rows, rank), BF16)] * steps
    outs += [shape((rank, n_cols), BF16), shape((rank, rank), BF16)]
    outs += [shape((n_cols // 2, rank), F32)] * 2 + [shape((8, rank), F32)]
    out = pl.pallas_call(
        functools.partial(factor_kernel, nx, ny, nz, cols_total),
        out_shape=outs,
        in_specs=[any_spec] * 3,
        out_specs=[any_spec] * len(outs),
        scratch_shapes=scratch,
        compiler_params=pltpu.CompilerParams(
            collective_id=0, has_side_effects=True, vmem_limit_bytes=51072 * 1024
        ),
        name="factors",
    )(gradient, momentum, right_factor)
    return pl.pallas_call(
        functools.partial(update_kernel, scaled),
        out_shape=[
            shape((n_rows, n_cols), BF16),
            shape((n_rows, n_cols), BF16),
            shape((n_cols, rank), F32),
        ],
        in_specs=[vm_spec] * (len(outs) + 1),
        out_specs=[any_spec] * 3,
        scratch_shapes=[
            vm((n_rows, n_cols), BF16),
            vm((n_rows, n_cols), BF16),
            vm((n_cols, rank), F32),
            dma((2 * steps + 1,)),
        ],
        compiler_params=pltpu.CompilerParams(vmem_limit_bytes=16 * 1024 * 1024),
        name="update",
    )(*out[: 2 * steps], weight, *out[2 * steps :])


def build(mesh, nx, ny, nz, cols_total, rows_total, rank):
    scaled = step_size * (rows_total / rank) ** 0.5
    return jax.shard_map(
        functools.partial(local, nx, ny, nz, cols_total, scaled),
        mesh=mesh,
        in_specs=(P("row", "col"), P("row", "col"), P("col", None), P("row", "col")),
        out_specs=(P("row", "col"), P("row", "col"), P("col", None)),
        check_vma=False,
    )


def solution(mesh):
    return build(mesh, NX, NY, mesh.shape["row"], COLS, ROWS, RANK)
```

time: 428 us -> 58.6 us (0.14)
  waiting for transfers between devices: 260 us -> 0 us
  blocking collectives: 67.2 us -> 0 us
  Pallas kernels: 0 us -> 57.9 us
  other arithmetic: 56.7 us -> 0 us
  matrix products: 23 us -> 0 us
  between operations: 15.2 us -> 0.65 us
  local copies, waits for them, and re-layouts: 5.16 us -> 0.01 us
    psum x3 -> x0, waiting for transfers between devices: 260 us -> none  [the longest x1 121 us: local(): left = lax.psum(partial_left, 'col')]
    psum x1 -> x0, blocking collectives: 67.2 us -> none  [local(): column_sums = lax.psum(jnp.sum(right * right, axis=0), 'col')]
    pallas_call x0 -> x2, Pallas kernels: none -> 57.9 us  [the longest x1 55.4 us: local(): pl.pallas_call(functools.partial(factor_kernel, nx, ny, nz, cols_total),...]
    another operation x9 -> x0, other arithmetic: 53.7 us -> none  [the longest x6 34 us: apply_lower(): lower = jnp.linalg.cholesky(gram)]
    dot_general x5 -> x0, matrix products: 18.6 us -> none  [the longest x1 6.38 us: contract_rows(): lax.dot_general(first, second, (((0,), (0,)), ((), ())), precision=lax.Pr...]
    another operation x5 -> x0, matrix products: 4.44 us -> none  [the longest x3 3.97 us: apply_lower(): lax.linalg.triangular_solve(lower, left, left_side=False, lower=True, tra...]
  transfers between devices with their start and end apart: 3 -> 0, of which waited for: 3 -> 0; matrix products, arithmetic and copies ran while one was open for 0% -> 0% of each run, Pallas kernels for 0% -> 0%
where the time goes in v2:
time: 58.6 us
  Pallas kernels  57.9 us (99%)
  between operations  0.65 us (1%)
    pallas_call x1, Pallas kernels, local(): pl.pallas_call(functools.partial(factor_kernel, nx, ny, nz, cols_total),...  55.4 us
    pallas_call x1, Pallas kernels, local(): pl.pallas_call(functools.partial(update_kernel, scaled), out_shape=[shape...  2.56 us

profile of v2, /device:TPU:1, one launch (start us, length us, event | category | flops | bytes accessed | tf_op | source)
XLA Modules:
  0.0 58.6 jit_solution(16987925692273784960)
XLA Ops:
  0.6 0.0 copy-start
  0.6 55.4 %factors.1 = (bf16[256,512]{1,0:T(8,128)(2,1)S(1)}, bf16[256,512]{1,0:T(8,128)(2,1)S(1)}, bf16[256,512]{1,0:T(8,128)(2,1)S(1)}, bf16[256,512]{1,0:T(8,128)(2,1)S...) custom-call(bf16[2048,512]{1,0:T(8,128)(2,1)} %g_hbm.1, ...), custom_call_target="tpu_custom_call" | custom-call | tf_op jit(solution)/shard_map/factors/pallas_call | solution.py:470
  56.0 0.0 copy-done
  56.0 2.6 %update.1 = (bf16[2048,512]{1,0:T(8,128)(2,1)}, bf16[2048,512]{1,0:T(8,128)(2,1)}, f32[512,256]{1,0:T(8,128)}) custom-call(bf16[256,512]{1,0:T(8,128)(2,1)S(1)} %get-tuple-element.24.refs_0_, bf16[256,512]{1,0:T(8,128)(2,1)S(1)} %get-tuple-element.25.refs_1_, bf16[256,512]{1,0:T(8,128)(2,1)S(1)} %get-tuple-element.26.refs_2_, ...), custom_call_target="tpu_custom_call" | custom-call | tf_op jit(solution)/shard_map/update/pallas_call | solution.py:481
Async XLA Ops:
  0.6 55.4 %copy-start = (bf16[2048,512]{1,0:T(8,128)(2,1)S(1)}, bf16[2048,512]{1,0:T(8,128)(2,1)}, u32[]{:S(2)}) copy-start(bf16[2048,512]{1,0:T(8,128)(2,1)} %refs_16_.1) | copy-start | bytes 6291460

commit v3 on v2

--- a/solution.py
+++ b/solution.py
@@ -42,56 +42,59 @@
     scale_row = lax.rsqrt(jnp.sum(diagonal, axis=0, keepdims=True))
     scale_col = lax.rsqrt(jnp.sum(diagonal, axis=1, keepdims=True))
     work_ref[:, :n] = gram * scale_row * scale_col
-    work_ref[:, n:] = jnp.where(rows == cols, 1.0, 0.0)
-
-    def block(j, carry):
-        start = pl.multiple_of(j * size, size)
-        outer = pl.multiple_of((j // (128 // size)) * 128, 128)
-        lead = work_ref[pl.ds(start, size), pl.ds(outer, 128)]
-        lead = pltpu.roll(lead, lax.rem(128 - (start - outer), 128), 1)
-        panel = work_ref[pl.ds(start, size), :]
-        tiles = [lead] + [panel[:, t * 128 : (t + 1) * 128] for t in range(2 * tiles_across)]
+
+    def block(start):
+        outer = start // 128 * 128
+        lead = work_ref[start : start + size, outer : outer + 128]
+        if start != outer:
+            lead = pltpu.roll(lead, 128 - (start - outer), 1)
+        panel = work_ref[start : start + size, :]
+        used = [t for t in range(tiles_across) if (t + 1) * 128 > start]
+        used += [tiles_across + t for t in range(tiles_across) if t * 128 < start + size]
+        tiles = [lead] + [panel[:, t * 128 : (t + 1) * 128] for t in used]
         done = []
         for first in range(0, size, group):
-            height = size - first
-            sub = lax.broadcasted_iota(jnp.int32, (height, 128), 0)
-            top = sub[:group]
             lead = tiles[0]
             columns = [
-                jnp.broadcast_to(lead[:, first + i : first + i + 1], (height, 128))
+                jnp.broadcast_to(lead[:, first + i : first + i + 1], (size - first, 128))
                 for i in range(group)
             ]
-            scale = jnp.ones((group, 128), F32)
-            for k in range(0, group, 2):
-                one, two = columns[k], columns[k + 1]
-                a = one[k : k + 1, :]
-                b = one[k + 1 : k + 2, :]
-                c = two[k + 1 : k + 2, :]
-                det = a * c - b * b
-                inv_a = 1.0 / a
-                inv_det = 1.0 / det
-                m1 = (one * c - two * b) * inv_det
-                m2 = (two * a - one * b) * inv_det
-                m1 = jnp.where(sub > k + 1, m1, jnp.where(sub == k + 1, b * inv_a, 0.0))
-                m2 = jnp.where(sub > k + 1, m2, 0.0)
-                scale = jnp.where(
-                    top == k,
-                    lax.rsqrt(a),
-                    jnp.where(top == k + 1, lax.rsqrt(det * inv_a), scale),
-                )
-                for i in range(k + 2, group):
-                    old = columns[i]
-                    columns[i] = old - m1 * old[k : k + 1, :] - m2 * old[k + 1 : k + 2, :]
-                tiles = [t - m1 * t[k : k + 1, :] - m2 * t[k + 1 : k + 2, :] for t in tiles]
-            done.append([t[:group] * scale for t in tiles[1:]])
-            tiles = [t[group:] for t in tiles]
-        tiles = [jnp.concatenate([d[t] for d in done], axis=0) for t in range(2 * tiles_across)]
+            for base in range(0, group, 8):
+                sub = lax.broadcasted_iota(jnp.int32, (size - first - base, 128), 0)
+                top = sub[:8]
+                scale = jnp.ones((8, 128), F32)
+                for k in range(0, 8, 2):
+                    one, two = columns[base + k], columns[base + k + 1]
+                    a = one[k : k + 1, :]
+                    b = one[k + 1 : k + 2, :]
+                    c = two[k + 1 : k + 2, :]
+                    det = a * c - b * b
+                    inv_a = 1.0 / a
+                    inv_det = 1.0 / det
+                    m1 = (one * c - two * b) * inv_det
+                    m2 = (two * a - one * b) * inv_det
+                    m1 = jnp.where(sub > k + 1, m1, jnp.where(sub == k + 1, b * inv_a, 0.0))
+                    m2 = jnp.where(sub > k + 1, m2, 0.0)
+                    scale = jnp.where(
+                        top == k,
+                        lax.rsqrt(a),
+                        jnp.where(top == k + 1, lax.rsqrt(det * inv_a), scale),
+                    )
+                    for i in range(base + k + 2, group):
+                        old = columns[i]
+                        columns[i] = old - m1 * old[k : k + 1, :] - m2 * old[k + 1 : k + 2, :]
+                    tiles = [t - m1 * t[k : k + 1, :] - m2 * t[k + 1 : k + 2, :] for t in tiles]
+                done.append([t[:8] * scale for t in tiles[1:]])
+                tiles = [t[8:] for t in tiles]
+                columns = [c[8:] if i >= base + 8 else c for i, c in enumerate(columns)]
+        found = {t: jnp.concatenate([d[i] for d in done], axis=0) for i, t in enumerate(used)}
+        empty = jnp.zeros((size, 128), F32)
+        tiles = [found.get(t, empty) for t in range(2 * tiles_across)]
         left = jnp.concatenate(tiles[:tiles_across], axis=1)
         right = jnp.concatenate(tiles[tiles_across:], axis=1)
-        out_ref[pl.ds(start, size), :] = right * scale_row
-
-        @pl.when(j < n // size - 1)
-        def _():
+        out_ref[start : start + size, :] = right * scale_row
+
+        if start + size < n:
             lane = lax.broadcasted_iota(jnp.int32, (size, n), 1)
             rest = jnp.where(lane >= start + size, left, 0.0)
             ph, pm, pq = split3(rest)
@@ -100,18 +103,18 @@
             rhs_g = jnp.concatenate([ph, pm, ph, pm, pq, ph], axis=0)
             rhs_x = jnp.concatenate([xh, xm, xh, xm, xq, xh], axis=0)
             rhs = jnp.concatenate([rhs_g, rhs_x], axis=1)
-            work_ref[...] -= lax.dot_general(
-                lhs, rhs, (((0,), (0,)), ((), ())), preferred_element_type=F32
+            under = (start + size) // 128 * 128
+            work_ref[under:, :] -= lax.dot_general(
+                lhs[:, under:], rhs, (((0,), (0,)), ((), ())), preferred_element_type=F32
             )
 
-        return carry
-
-    lax.fori_loop(0, n // size, block, 0)
+    for start in range(0, n, size):
+        block(start)
 
 
 def factor_kernel(nx, ny, nz, cols_total, g_hbm, m_hbm, v_hbm, *refs):
-    b_outs, l_outs, refs = refs[:steps], refs[steps : 2 * steps], refs[2 * steps :]
-    z1_out, xt_out, r_out, r2_out, scale_out, g_v, m_v, v_v, b_v, xs, xr, s_v, sa, ra, la, *refs = refs
+    nm_outs, l_outs, refs = refs[:steps], refs[steps : 2 * steps], refs[2 * steps :]
+    xt_out, r_out, r2_out, scale_out, g_v, m_v, v_v, b_v, xs, xr, s_v, sa, ra, la, *refs = refs
     lt, gfull, gz, gall, wacc, wh, wr, wg, work, inv, cs, z1, xt, right, scale_v, *refs = refs
     load_sem, out_sem, pair_s, pair_r, rs_s, rs_r, ag_s, ag_r, fw_s, fw_r, *refs = refs
     gz_s, gz_r, gp_s, gp_r, wr_s, wr_r, wg_s, wg_r, cs_s, cs_r = refs
@@ -148,20 +151,6 @@
         sent.append(copy)
         return copy
 
-    barrier = pltpu.get_barrier_semaphore()
-
-    def greet_plane(d, carry):
-        to = {"row": z, "col": lax.rem(p + d, plane)}
-        pl.semaphore_signal(barrier, inc=1, device_id=to, device_id_type=MESH)
-        return carry
-
-    def greet_line(d, carry):
-        to = {"row": lax.rem(z + d, nz), "col": p}
-        pl.semaphore_signal(barrier, inc=1, device_id=to, device_id_type=MESH)
-        return carry
-
-    lax.fori_loop(1, plane, greet_plane, 0)
-    lax.fori_loop(1, nz, greet_line, 0)
     v_load = pltpu.make_async_copy(v_hbm, v_v, load_sem.at[0])
     v_load.start()
     offsets = [(1 - core) * half + h * piece for h in range(n_pieces)]
@@ -177,6 +166,26 @@
         for c in pair:
             c.start()
         loads.append(pair)
+    barrier = pltpu.get_barrier_semaphore()
+
+    def ring(here, d, size):
+        to = here + d
+        return jnp.where(to >= size, to - size, to)
+
+    def greet_plane(d, carry):
+        to = {"row": z, "col": ring(p, d, plane)}
+        pl.semaphore_signal(barrier, inc=1, device_id=to, device_id_type=MESH)
+        return carry
+
+    def greet_line(d, carry):
+        to = {"row": ring(z, d, nz), "col": p}
+        pl.semaphore_signal(barrier, inc=1, device_id=to, device_id_type=MESH)
+        return carry
+
+    for d in range(1, nz):
+        greet_line(d, 0)
+    for d in range(1, plane):
+        greet_plane(d, 0)
     v_load.wait()
     factor_half = v_v[...].astype(BF16)
 
@@ -190,6 +199,9 @@
 
     for h in range(n_pieces):
         xs[h] = product(h).astype(BF16)
+    for h in range(n_pieces):
+        s_v[h] = product(n_pieces + h).reshape(chips, piece_rows, rank)
+        ra[h, q] = jnp.zeros((piece_rows, rank), BF16)
     pl.semaphore_wait(barrier, plane - 1 + nz - 1)
     pairs = []
     for h in range(n_pieces):
@@ -197,24 +209,22 @@
 
     def spread_piece(h):
         def to_chip(d, carry):
-            to = lax.rem(q + d, chips)
+            to = ring(q, d, chips)
             copy_to(sa.at[h, to], ra.at[h, q], rs_s.at[h], rs_r.at[h], at(to, core)).start()
             return carry
 
         lax.fori_loop(1, chips, to_chip, 0)
 
     for h in range(n_pieces):
-        own = product(n_pieces + h)
-        ra[h, q] = jnp.zeros((piece_rows, rank), BF16)
         pairs[h].wait_recv()
-        total = (own + xr[h].astype(F32)).reshape(chips, piece_rows, rank)
+        total = s_v[h] + xr[h].astype(F32).reshape(chips, piece_rows, rank)
         s_v[h] = total
         sa[h] = total.astype(BF16)
         spread_piece(h)
 
     def gather_piece(h):
         def to_chip(d, carry):
-            to = lax.rem(q + d, chips)
+            to = ring(q, d, chips)
             here = la.at[core, h, q]
             copy_to(here, here, ag_s.at[h], ag_r.at[h], at(to, core)).start()
             return carry
@@ -269,7 +279,7 @@
     gz[z] = gfull[mine, :]
     gz_c = []
     for d in range(1, nz):
-        to = {"row": lax.rem(z + d, nz), "col": p}
+        to = {"row": ring(z, d, nz), "col": p}
         gz_c.append(send(gz.at[z], gz.at[z], gz_s.at[d - 1], gz_r.at[d - 1], to))
 
     accumulate_right(n_pieces - 1)
@@ -281,7 +291,7 @@
     for h in range(sum_pieces):
         wr[h, z] = wh[z, h]
         for d in range(1, nz):
-            to = lax.rem(z + d, nz)
+            to = ring(z, d, nz)
             sems = wr_s.at[h, d - 1], wr_r.at[h, d - 1]
             wr_c.append(send(wh.at[to, h], wr.at[h, z], *sems, {"row": to, "col": p}))
     outs = []
@@ -291,8 +301,6 @@
         chip = (i * rows % piece) // piece_rows
         source = la.at[c, h, pl.ds(chip, rows // piece_rows)]
         outs.append(pltpu.make_async_copy(source, l_outs[i], out_sem.at[2 * i]))
-        source = b_v.at[pl.ds(i * rows, rows)]
-        outs.append(pltpu.make_async_copy(source, b_outs[i], out_sem.at[2 * i + 1]))
     for c in outs:
         c.start()
 
@@ -304,7 +312,7 @@
     gall[mine, :] = acc
 
     def spread(d, carry):
-        to = {"row": z, "col": lax.rem(p + d, plane)}
+        to = {"row": z, "col": ring(p, d, plane)}
         copy_to(gall.at[mine], gall.at[mine], gp_s, gp_r, to).start()
         return carry
 
@@ -319,18 +327,17 @@
             acc = acc + wr[h, i].astype(F32)
         wg[z, h] = acc.astype(BF16)
         for d in range(1, nz):
-            to = {"row": lax.rem(z + d, nz), "col": p}
+            to = {"row": ring(z, d, nz), "col": p}
             sems = wg_s.at[h, d - 1], wg_r.at[h, d - 1]
             wg_c.append(send(wg.at[z, h], wg.at[z, h], *sems, to))
 
     others = gall.at[pl.ds(0, (plane - 1) * share)]
+    at_row = lax.broadcasted_iota(jnp.int32, (rank, rank), 0)
+    at_col = lax.broadcasted_iota(jnp.int32, (rank, rank), 1)
+    work[:, rank:] = jnp.where(at_row == at_col, 1.0, 0.0)
     all_gram = copy_to(others, others, gp_s, gp_r, at(q, 1 - core))
     all_gram.wait_recv()
     inverse_factor(gall, work, inv)
-    inv_t = inv[...].T.astype(BF16)
-    xt[...] = inv_t
-    outs.append(pltpu.make_async_copy(xt, xt_out, out_sem.at[2 * steps]))
-    outs[-1].start()
 
     for c in wg_c:
         c.wait_recv()
@@ -346,25 +353,36 @@
     sums = lax.dot_general(ones, sq_h, dims, preferred_element_type=F32) + lax.dot_general(
         ones, sq_m, dims, preferred_element_type=F32
     )
-    upper = lax.broadcasted_iota(jnp.int32, (8, half_rank), 0) < 4
-    cs[p] = jnp.where(upper, sums[:, :half_rank], sums[:, half_rank:])
+    cs[p] = jnp.concatenate([sums[0:1, :half_rank], sums[0:1, half_rank:]], axis=0)
 
     def spread_sums(d, carry):
-        to = {"row": z, "col": lax.rem(p + d, plane)}
+        to = {"row": z, "col": ring(p, d, plane)}
         copy_to(cs.at[p], cs.at[p], cs_s, cs_r, to).start()
         return carry
 
     lax.fori_loop(1, plane, spread_sums, 0)
+    inv_t = inv[...].T.astype(BF16)
+    xt[...] = inv_t
     z1[...] = jnp.dot(inv_t, right_t.astype(BF16), preferred_element_type=F32).astype(BF16)
     right[...] = right_t.T
     mid = n_cols // 2
     outs += [
-        pltpu.make_async_copy(z1, z1_out, out_sem.at[2 * steps + 1]),
+        pltpu.make_async_copy(xt, xt_out, out_sem.at[2 * steps + 1]),
         pltpu.make_async_copy(right.at[pl.ds(0, mid)], r_out, out_sem.at[2 * steps + 2]),
         pltpu.make_async_copy(right.at[pl.ds(mid, mid)], r2_out, out_sem.at[2 * steps + 3]),
     ]
     for c in outs[-3:]:
         c.start()
+    rows = b_v.shape[0] // steps
+    for i in range(steps):
+        c, h = i * rows // half, (i * rows % half) // piece
+        chip = (i * rows % piece) // piece_rows
+        part = pl.ds(i * rows, rows)
+        left = la[c, h, chip : chip + rows // piece_rows].reshape(rows, rank)
+        projection = jnp.dot(left, z1[...], preferred_element_type=F32)
+        b_v[part, :] = (b_v[part, :].astype(F32) - (1.0 - momentum_keep) * projection).astype(BF16)
+        outs.append(pltpu.make_async_copy(b_v.at[part], nm_outs[i], out_sem.at[2 * i + 1]))
+        outs[-1].start()
     for c in sent + waits + [all_gram]:
         c.wait_send()
     other_sums = cs.at[pl.ds(0, plane - 1)]
@@ -374,7 +392,7 @@
     for i in range(1, plane):
         acc = acc + cs[i]
     acc = lax.rsqrt(acc / cols_total + 1e-06)
-    scale = jnp.concatenate([acc[0:1, :], acc[4:5, :]], axis=1)
+    scale = jnp.concatenate([acc[0:1, :], acc[1:2, :]], axis=1)
     scale_v[...] = jnp.broadcast_to(scale, scale_v.shape)
     outs.append(pltpu.make_async_copy(scale_v, scale_out, out_sem.at[2 * steps + 4]))
     outs[-1].start()
@@ -384,15 +402,20 @@
 
 
 def update_kernel(scaled, *refs):
-    b_refs, l_refs, refs = refs[:steps], refs[steps : 2 * steps], refs[2 * steps :]
-    w_ref, z1_ref, xt_ref, r_ref, r2_ref, scale_ref, nw_hbm, nm_hbm, nf_hbm, nw, nm, nf, sems = refs
+    nm_refs, l_refs, refs = refs[:steps], refs[steps : 2 * steps], refs[2 * steps :]
+    w_ref, xt_ref, r_ref, r2_ref, scale_ref, nw_hbm, nm_hbm, nf_hbm, nw, nf, sems = refs
     block = nw.shape[0] // steps
     mid = r_ref.shape[0]
+    copies = []
+    for i in range(steps):
+        part = pl.ds(i * block, block)
+        copies.append(pltpu.make_async_copy(nm_refs[i], nm_hbm.at[part], sems.at[2 * i]))
+        copies[-1].start()
     scale = scale_ref[0:1, :]
     nf[:mid, :] = r_ref[...] * scale
     nf[mid:, :] = r2_ref[...] * scale
-    copies = [pltpu.make_async_copy(nf, nf_hbm, sems.at[2 * steps])]
-    copies[0].start()
+    copies.append(pltpu.make_async_copy(nf, nf_hbm, sems.at[2 * steps]))
+    copies[-1].start()
     z2 = lax.dot_general(
         xt_ref[...],
         nf[...].astype(BF16),
@@ -402,10 +425,6 @@
     for i in range(steps):
         part = pl.ds(i * block, block)
         left = l_refs[i][...].reshape(block, z2.shape[0])
-        projection = jnp.dot(left, z1_ref[...], preferred_element_type=F32)
-        nm[part, :] = (b_refs[i][...].astype(F32) - (1.0 - momentum_keep) * projection).astype(BF16)
-        copies.append(pltpu.make_async_copy(nm.at[part], nm_hbm.at[part], sems.at[2 * i]))
-        copies[-1].start()
         direction = jnp.dot(left, z2, preferred_element_type=F32)
         nw[part, :] = (w_ref[part, :].astype(F32) - scaled * direction).astype(BF16)
         copies.append(pltpu.make_async_copy(nw.at[part], nw_hbm.at[part], sems.at[2 * i + 1]))
@@ -452,7 +471,7 @@
         vm((nz, sum_pieces, part, n_cols), BF16),
         vm((rank, 2 * rank), F32),
         vm((rank, rank), F32),
-        vm((plane, 8, rank // 2), F32),
+        vm((plane, 2, rank // 2), F32),
         vm((rank, n_cols), BF16),
         vm((rank, rank), BF16),
         vm((n_cols, rank), F32),
@@ -465,7 +484,7 @@
     scratch += [dma((sum_pieces, nz - 1))] * 4 + [dma, dma]
     outs = [shape((block, n_cols), BF16)] * steps
     outs += [shape((block // piece_rows, piece_rows, rank), BF16)] * steps
-    outs += [shape((rank, n_cols), BF16), shape((rank, rank), BF16)]
+    outs += [shape((rank, rank), BF16)]
     outs += [shape((n_cols // 2, rank), F32)] * 2 + [shape((8, rank), F32)]
     out = pl.pallas_call(
         functools.partial(factor_kernel, nx, ny, nz, cols_total),
@@ -474,7 +493,7 @@
         out_specs=[any_spec] * len(outs),
         scratch_shapes=scratch,
         compiler_params=pltpu.CompilerParams(
-            collective_id=0, has_side_effects=True, vmem_limit_bytes=51072 * 1024
+            collective_id=0, has_side_effects=True, vmem_limit_bytes=51328 * 1024
         ),
         name="factors",
     )(gradient, momentum, right_factor)
@@ -489,7 +508,6 @@
         out_specs=[any_spec] * 3,
         scratch_shapes=[
             vm((n_rows, n_cols), BF16),
-            vm((n_rows, n_cols), BF16),
             vm((n_cols, rank), F32),
             dma((2 * steps + 1,)),
         ],

time: 58.6 us -> 57.7 us (0.985)
  Pallas kernels: 57.9 us -> 56.9 us
    pallas_call x1, Pallas kernels: 55.4 us -> 54.6 us  [local(): pl.pallas_call(functools.partial(factor_kernel, nx, ny, nz, cols_total),...]
where the time goes in v3:
time: 57.7 us; the launch traced here: 57.6 us
  Pallas kernels  56.9 us (99%)
  between operations  0.65 us (1%)
    pallas_call x1, Pallas kernels, local(): pl.pallas_call(functools.partial(factor_kernel, nx, ny, nz, cols_total),...  54.6 us
    pallas_call x1, Pallas kernels, local(): pl.pallas_call(functools.partial(update_kernel, scaled), out_shape=[shape...  2.32 us

profile of v3, /device:TPU:1, one launch (start us, length us, event | category | flops | bytes accessed | tf_op | source)
XLA Modules:
  0.0 57.6 jit_solution(17927032400461636156)
XLA Ops:
  0.6 0.0 copy-start
  0.6 54.6 %factors.1 = (bf16[256,512]{1,0:T(8,128)(2,1)S(1)}, bf16[256,512]{1,0:T(8,128)(2,1)S(1)}, bf16[256,512]{1,0:T(8,128)(2,1)S(1)}, bf16[256,512]{1,0:T(8,128)(2,1)S...) custom-call(bf16[2048,512]{1,0:T(8,128)(2,1)} %g_hbm.1, ...), custom_call_target="tpu_custom_call" | custom-call | tf_op jit(solution)/shard_map/factors/pallas_call | solution.py:489
  55.2 0.0 copy-done
  55.3 2.3 %update.1 = (bf16[2048,512]{1,0:T(8,128)(2,1)}, bf16[2048,512]{1,0:T(8,128)(2,1)}, f32[512,256]{1,0:T(8,128)}) custom-call(bf16[256,512]{1,0:T(8,128)(2,1)S(1)} %get-tuple-element.23.refs_0_, bf16[256,512]{1,0:T(8,128)(2,1)S(1)} %get-tuple-element.24.refs_1_, bf16[256,512]{1,0:T(8,128)(2,1)S(1)} %get-tuple-element.25.refs_2_, ...), custom_call_target="tpu_custom_call" | custom-call | tf_op jit(solution)/shard_map/update/pallas_call | solution.py:500
Async XLA Ops:
  0.6 54.6 %copy-start = (bf16[2048,512]{1,0:T(8,128)(2,1)S(1)}, bf16[2048,512]{1,0:T(8,128)(2,1)}, u32[]{:S(2)}) copy-start(bf16[2048,512]{1,0:T(8,128)(2,1)} %refs_16_.1) | copy-start | bytes 6291460

commit v4 on v3

--- a/solution.py
+++ b/solution.py
@@ -168,12 +168,20 @@
         loads.append(pair)
     barrier = pltpu.get_barrier_semaphore()
 
+    line_order = sorted(range(1, nz), key=lambda d: -min(d, nz - d))
+    plane_far = (nx // 2 * ny + ny // 2) * CORES - 1
+    chip_far = nx // 2 * ny + ny // 2 - 1
+
+    def from_far(i, far, size):
+        d = i + far
+        return jnp.where(d >= size, d - (size - 1), d)
+
     def ring(here, d, size):
         to = here + d
         return jnp.where(to >= size, to - size, to)
 
     def greet_plane(d, carry):
-        to = {"row": z, "col": ring(p, d, plane)}
+        to = {"row": z, "col": ring(p, from_far(d, plane_far, plane), plane)}
         pl.semaphore_signal(barrier, inc=1, device_id=to, device_id_type=MESH)
         return carry
 
@@ -182,7 +190,7 @@
         pl.semaphore_signal(barrier, inc=1, device_id=to, device_id_type=MESH)
         return carry
 
-    for d in range(1, nz):
+    for d in line_order:
         greet_line(d, 0)
     for d in range(1, plane):
         greet_plane(d, 0)
@@ -209,7 +217,7 @@
 
     def spread_piece(h):
         def to_chip(d, carry):
-            to = ring(q, d, chips)
+            to = ring(q, from_far(d, chip_far, chips), chips)
             copy_to(sa.at[h, to], ra.at[h, q], rs_s.at[h], rs_r.at[h], at(to, core)).start()
             return carry
 
@@ -224,7 +232,7 @@
 
     def gather_piece(h):
         def to_chip(d, carry):
-            to = ring(q, d, chips)
+            to = ring(q, from_far(d, chip_far, chips), chips)
             here = la.at[core, h, q]
             copy_to(here, here, ag_s.at[h], ag_r.at[h], at(to, core)).start()
             return carry
@@ -270,15 +278,14 @@
         forwards.append(send(here, here, fw_s.at[h], fw_r.at[h], at(q, 1 - core)))
         if h > 0:
             accumulate(h - 1)
-    for h in range(n_pieces - 1):
-        accumulate_right(h)
+            accumulate_right(h - 1)
     accumulate(n_pieces - 1)
 
     share = rank // plane
     mine = pl.ds(pl.multiple_of(p * share, share), share)
     gz[z] = gfull[mine, :]
     gz_c = []
-    for d in range(1, nz):
+    for d in line_order:
         to = {"row": ring(z, d, nz), "col": p}
         gz_c.append(send(gz.at[z], gz.at[z], gz_s.at[d - 1], gz_r.at[d - 1], to))
 
@@ -290,7 +297,7 @@
     wr_c = []
     for h in range(sum_pieces):
         wr[h, z] = wh[z, h]
-        for d in range(1, nz):
+        for d in line_order:
             to = ring(z, d, nz)
             sems = wr_s.at[h, d - 1], wr_r.at[h, d - 1]
             wr_c.append(send(wh.at[to, h], wr.at[h, z], *sems, {"row": to, "col": p}))
@@ -312,7 +319,7 @@
     gall[mine, :] = acc
 
     def spread(d, carry):
-        to = {"row": z, "col": ring(p, d, plane)}
+        to = {"row": z, "col": ring(p, from_far(d, plane_far, plane), plane)}
         copy_to(gall.at[mine], gall.at[mine], gp_s, gp_r, to).start()
         return carry
 
@@ -326,7 +333,7 @@
         for i in range(1, nz):
             acc = acc + wr[h, i].astype(F32)
         wg[z, h] = acc.astype(BF16)
-        for d in range(1, nz):
+        for d in line_order:
             to = {"row": ring(z, d, nz), "col": p}
             sems = wg_s.at[h, d - 1], wg_r.at[h, d - 1]
             wg_c.append(send(wg.at[z, h], wg.at[z, h], *sems, to))
@@ -356,7 +363,7 @@
     cs[p] = jnp.concatenate([sums[0:1, :half_rank], sums[0:1, half_rank:]], axis=0)
 
     def spread_sums(d, carry):
-        to = {"row": z, "col": ring(p, d, plane)}
+        to = {"row": z, "col": ring(p, from_far(d, plane_far, plane), plane)}
         copy_to(cs.at[p], cs.at[p], cs_s, cs_r, to).start()
         return carry
 

time: 57.7 us -> 56.5 us (0.979)
  Pallas kernels: 56.9 us -> 55.8 us
    pallas_call x1, Pallas kernels: 54.6 us -> 53.5 us  [local(): pl.pallas_call(functools.partial(factor_kernel, nx, ny, nz, cols_total),...]
where the time goes in v4:
time: 56.5 us; the launch traced here: 56.4 us
  Pallas kernels  55.8 us (99%)
  between operations  0.65 us (1%)
    pallas_call x1, Pallas kernels, local(): pl.pallas_call(functools.partial(factor_kernel, nx, ny, nz, cols_total),...  53.5 us
    pallas_call x1, Pallas kernels, local(): pl.pallas_call(functools.partial(update_kernel, scaled), out_shape=[shape...  2.32 us

profile of v4, /device:TPU:1, one launch (start us, length us, event | category | flops | bytes accessed | tf_op | source)
XLA Modules:
  0.0 56.4 jit_solution(10294770376397252189)
XLA Ops:
  0.6 0.0 copy-start
  0.6 53.5 %factors.1 = (bf16[256,512]{1,0:T(8,128)(2,1)S(1)}, bf16[256,512]{1,0:T(8,128)(2,1)S(1)}, bf16[256,512]{1,0:T(8,128)(2,1)S(1)}, bf16[256,512]{1,0:T(8,128)(2,1)S...) custom-call(bf16[2048,512]{1,0:T(8,128)(2,1)} %g_hbm.1, ...), custom_call_target="tpu_custom_call" | custom-call | tf_op jit(solution)/shard_map/factors/pallas_call | solution.py:496
  54.1 0.0 copy-done
  54.1 2.3 %update.1 = (bf16[2048,512]{1,0:T(8,128)(2,1)}, bf16[2048,512]{1,0:T(8,128)(2,1)}, f32[512,256]{1,0:T(8,128)}) custom-call(bf16[256,512]{1,0:T(8,128)(2,1)S(1)} %get-tuple-element.23.refs_0_, bf16[256,512]{1,0:T(8,128)(2,1)S(1)} %get-tuple-element.24.refs_1_, bf16[256,512]{1,0:T(8,128)(2,1)S(1)} %get-tuple-element.25.refs_2_, ...), custom_call_target="tpu_custom_call" | custom-call | tf_op jit(solution)/shard_map/update/pallas_call | solution.py:507
Async XLA Ops:
  0.6 53.5 %copy-start = (bf16[2048,512]{1,0:T(8,128)(2,1)S(1)}, bf16[2048,512]{1,0:T(8,128)(2,1)}, u32[]{:S(2)}) copy-start(bf16[2048,512]{1,0:T(8,128)(2,1)} %refs_16_.1) | copy-start | bytes 6291460
